TPU v7x, 32 devices: a whole 2x2x4 slice. The times are simulated.
32 devices in a mesh: expert: 8 (over z, x), half: 4 (over y, core).
Axes of the slice: x: 2, y: 2, z: 4, core: 2. Of those that a mesh axis runs over, the one named last changes fastest.
Arguments:
- tokens: bfloat16 [8192, 1024], P(('expert', 'half')), may hold values from -6 to 6
- router: bfloat16 [1024, 16], replicated, may hold values from -1 to 1
- w_in: bfloat16 [8, 1024, 3072], P('expert', None, 'half'), may hold values from -0.1875 to 0.1875
- w_out: bfloat16 [8, 3072, 1024], P('expert', 'half'), may hold values from -0.109375 to 0.109375
Outputs:
- mixed: bfloat16 [8192, 1024], P(('expert', 'half'))
All inputs are finite; a program needn't handle non-finite values.
Results may differ from a plain program's by a relative error of at most 0.018.
Values may be sent and summed in bfloat16 or wider, within the bound.
A program may use at most 64 MiB of HBM per device.

v0:
```python
import jax
import jax.numpy as jnp
from jax import lax
from jax.sharding import PartitionSpec as P

SLOTS = 2
PATCHES = 256


def expert_quarter(rows, first, second):
    hidden = jax.nn.gelu(
        jnp.einsum("erd,edf->erf", rows, first, preferred_element_type=jnp.float32)
    ).astype(jnp.bfloat16)
    return jnp.einsum("erf,efd->erd", hidden, second, preferred_element_type=jnp.float32)


def on_device(tokens, router, w_in, w_out):
    width = tokens.shape[1]
    images = tokens.shape[0] // PATCHES
    experts_all = router.shape[1] // SLOTS
    picture = tokens.reshape(images, PATCHES, width)
    logits = jnp.einsum("imd,dc->imc", picture, router, preferred_element_type=jnp.float32)
    dispatch = jax.nn.softmax(logits, axis=1).astype(jnp.bfloat16)
    combine = jax.nn.softmax(logits, axis=2).astype(jnp.bfloat16)
    slot_input = jnp.einsum(
        "imc,imd->icd", dispatch, picture, preferred_element_type=jnp.float32
    ).astype(jnp.bfloat16)
    outgoing = slot_input.reshape(images, experts_all, SLOTS, width)
    arrived = lax.all_to_all(outgoing, "expert", split_axis=1, concat_axis=0, tiled=True)
    local_experts = arrived.shape[1]
    slot_rows_local = jnp.transpose(arrived, (1, 0, 2, 3)).reshape(local_experts, -1, width)
    terms = expert_quarter(lax.all_gather(slot_rows_local, "half", axis=1, tiled=True), w_in, w_out)
    result = lax.psum_scatter(terms.astype(jnp.bfloat16), "half", scatter_dimension=1, tiled=True)
    back = jnp.transpose(result.reshape(local_experts, -1, SLOTS, width), (1, 0, 2, 3))
    returned = lax.all_to_all(back, "expert", split_axis=0, concat_axis=1, tiled=True)
    slot_output = returned.reshape(images, experts_all * SLOTS, width)
    mixed = jnp.einsum(
        "imc,icd->imd", combine, slot_output, preferred_element_type=jnp.float32
    ).astype(jnp.bfloat16)
    return mixed.reshape(-1, width)


def solution(mesh):
    return jax.shard_map(
        on_device,
        mesh=mesh,
        in_specs=(
            P(("expert", "half"), None),
            P(),
            P("expert", None, "half"),
            P("expert", "half", None),
        ),
        out_specs=P(("expert", "half"), None),
        check_vma=False,
    )
```

profile of v0, /device:TPU:0, one launch (start us, length us, event | category | flops | bytes accessed | tf_op | source)
XLA Modules:
  0.0 69.6 jit_solution(18118981215828723540)
XLA Ops:
  6.5 0.0 copy-start
  6.5 0.0 reduce-scatter.2.cloned.1.call-start
  6.5 1.5 %fusion.40 = (f32[256]{0:T(256)S(1)}, f32[16]{0:T(128)S(1)}, f32[256,16]{0,1:T(8,128)S(1)}) fusion(bf16[256,1024]{1,0:T(8,128)(2,1)} %param.4, bf16[1024,16]{0,1:T(8,128)(2,1)} %param.5), kind=kOutput, calls=%fused_computation.36 | convolution fusion | flops 8396528 | bytes 574528 | tf_op jit(solution)/shard_map/imd,dc->imc/dot_general | solution.py:22
  8.1 0.2 fusion.30
  8.3 1.3 %convolution_convert_fusion.1 = bf16[16,1024]{1,0:T(8,128)(2,1)S(1)} fusion(bf16[256,1024]{1,0:T(8,128)(2,1)} %param.4, f32[256,16]{0,1:T(8,128)S(1)} %get-tuple-element.9, f32[16]{0:T(128)S(1)} %get-tuple-element.6, f32[16]{0:T(128)S(1)} %get-tuple-element.8), kind=kOutput, calls=%fused_computation.7 | convolution fusion | flops 8417280 | bytes 573568 | tf_op jit(solution)/shard_map/imc,imd->icd/dot_general | solution.py:25
  9.6 13.7 %all_to_all.8 = bf16[1,8,2,1024]{3,2,0,1:T(2,128)(2,1)S(1)} all-to-all(bf16[1,8,2,1024]{3,2,0,1:T(2,128)(2,1)S(1)} %bitcast.30), channel_id=1, replica_groups=mesh['expert'=8,'half'=4] {'expert'}, dimensions={1} | all-to-all | bytes 65536 | tf_op jit(solution)/shard_map/all_to_all | solution.py:29
  23.3 5.4 %all_gather.3 = bf16[1,64,1024]{2,1,0:T(8,128)(2,1)S(1)} all-gather(bf16[1,16,1024]{2,1,0:T(8,128)(2,1)S(1)} %reshape_transpose.3), channel_id=1, replica_groups=mesh['expert'=8,'half'=4] {'half'}, dimensions={1}, use_global_device_ids=true | all-gather | bytes 163840 | tf_op jit(solution)/shard_map/all_gather | solution.py:32
  28.8 0.0 copy-done
  28.8 2.9 %fusion.7 = bf16[1,64,1024]{2,1,0:T(8,128)(2,1)} fusion(bf16[1,768,1024]{2,1,0:T(8,128)(2,1)S(1)} %copy-done, bf16[1,1024,768]{2,1,0:T(8,128)(2,1)} %param.6, bf16[1,64,1024]{2,1,0:T(8,128)(2,1)S(1)} %all_gather.3), kind=kOutput, calls=%fused_computation.6 | convolution fusion | flops 201834496 | bytes 3407872 | tf_op jit(solution)/shard_map/erf,efd->erd/dot_general | solution.py:14
  31.7 0.0 reduce-scatter.2.cloned.1.call-update
  31.7 17.2 %reduce-scatter.2.cloned.1.call-done = bf16[1,16,1024]{2,1,0:T(8,128)(2,1)} async-done(((bf16[1,64,1024]{2,1,0:T(8,128)(2,1)}), bf16[1,16,1024]{2,1,0:T(8,128)(2,1)}) %reduce-scatter.2.cloned.1.call-update) | async-done | bytes 32784 | tf_op jit(solution)/shard_map/reduce_scatter | solution.py:33
  48.9 0.8 %transpose_reshape.3 = bf16[8,1,2,1024]{3,2,0,1:T(2,128)(2,1)S(1)} reshape(bf16[1,16,1024]{2,1,0:T(8,128)(2,1)} %reduce-scatter.2.cloned.1.call-done) | data formatting | bytes 65536 | tf_op jit(solution)/shard_map/transpose;reshape | solution.py:34
  49.6 12.0 %all_to_all.9 = bf16[8,1,2,1024]{3,2,1,0:T(2,128)(2,1)S(1)} all-to-all(bf16[8,1,2,1024]{3,2,1,0:T(2,128)(2,1)S(1)} %bitcast.31), channel_id=1, replica_groups=mesh['expert'=8,'half'=4] {'expert'}, dimensions={0} | all-to-all | bytes 65536 | tf_op jit(solution)/shard_map/all_to_all | solution.py:35
  61.7 1.1 %convolution_convert_fusion = bf16[256,1024]{1,0:T(8,128)(2,1)} fusion(bf16[16,1024]{1,0:T(8,128)(2,1)S(1)} %reshape.89, f32[256,16]{0,1:T(8,128)S(1)} %get-tuple-element.9, f32[256]{0:T(256)S(1)} %get-tuple-element.5, f32[256]{0:T(256)S(1)} %get-tuple-element.7), kind=kOutput, calls=%fused_computation.4 | convolution fusion | flops 8663040 | bytes 575488 | tf_op jit(solution)/shard_map/imc,icd->imd/dot_general | solution.py:37
  (3 shorter events, 0.1 us)
Async XLA Ops:
  6.5 22.2 %copy-start = (bf16[1,768,1024]{2,1,0:T(8,128)(2,1)S(1)}, bf16[1,768,1024]{2,1,0:T(8,128)(2,1)}, u32[]{:S(2)}) copy-start(bf16[1,768,1024]{2,1,0:T(8,128)(2,1)} %param.7) | copy-start | bytes 4718596
  6.5 42.3 %reduce-scatter.2.cloned.1.call-start = ((), (), s32[]{:S(2)}) async-start(), calls=%async_computation.3 | async-start | bytes 163840 | tf_op jit(solution)/shard_map/reduce_scatter | solution.py:33
Sparse Core Ops, SparseCore 0:
  31.8 17.0 reduce-scatter.1
where the time goes:
time: 70 us; the launch traced here: 69.6 us
  blocking collectives  31.2 us (45%)
  waiting for transfers between devices  17.2 us (25%)
  between operations  13.4 us (19%)
  matrix products  6.84 us (10%)
  local copies, waits for them, and re-layouts  0.84 us (1%)
    reduce_scatter x1, waiting for transfers between devices, on_device(): lax.psum_scatter(terms.astype(jnp.bfloat16), 'half', scatter_dimension=1,...  17.2 us
    all_to_all x1, blocking collectives, on_device(): lax.all_to_all(outgoing, 'expert', split_axis=1, concat_axis=0, tiled=True)  13.7 us
    all_to_all x1, blocking collectives, on_device(): lax.all_to_all(back, 'expert', split_axis=0, concat_axis=1, tiled=True)  12 us
    all_gather x1, blocking collectives, on_device(): lax.all_gather(slot_rows_local, 'half', axis=1, tiled=True)  5.43 us
    dot_general x1, matrix products, expert_quarter(): jnp.einsum('erf,efd->erd', hidden, second, preferred_element_type=jnp.flo...  2.91 us
    dot_general x1, matrix products, on_device(): jnp.einsum('imd,dc->imc', picture, router, preferred_element_type=jnp.flo...  1.53 us
  transfers between devices with their start and end apart: 1, of which 1 were waited for; matrix products, arithmetic and copies ran while one was open for 0% of the time, Pallas kernels for 0%

commit v1 on v0

v1 whole, which is shorter than its diff:
```python
import functools

import jax
import jax.numpy as jnp
from jax import lax
from jax.experimental import pallas as pl
from jax.experimental.pallas import tpu as pltpu
from jax.sharding import PartitionSpec as P

SLOTS = 2
LANES = 128
MESH = pl.DeviceIdType.MESH
F32 = jnp.float32
BF16 = jnp.bfloat16


def swap_matrix(blocks):
    size = blocks * blocks * SLOTS
    row = lax.broadcasted_iota(jnp.int32, (size, size), 0)
    column = lax.broadcasted_iota(jnp.int32, (size, size), 1)
    line = blocks * SLOTS
    a, b, s = row // line, (row % line) // SLOTS, row % SLOTS
    return jnp.where(column == b * line + a * SLOTS + s, 1.0, 0.0).astype(BF16)


def to_messages(swap, rows, blocks):
    line = blocks * SLOTS
    groups = rows.shape[0] // line
    stacked = [
        jnp.concatenate(
            [
                rows[g * line:(g + 1) * line, j * LANES:(j + 1) * LANES]
                for j in range(blocks)
            ],
            axis=0,
        )
        for g in range(groups)
    ]
    moved = jnp.dot(swap, jnp.concatenate(stacked, axis=1), preferred_element_type=F32).astype(BF16)
    return [
        moved[:, g * LANES:(g + 1) * LANES].reshape(blocks, line, LANES) for g in range(groups)
    ]


def to_rows(swap, tiles, blocks):
    line = blocks * SLOTS
    groups = tiles.shape[0] // blocks
    stacked = jnp.concatenate(
        [
            tiles[g * blocks:(g + 1) * blocks].reshape(blocks * line, LANES)
            for g in range(groups)
        ],
        axis=1,
    )
    moved = jnp.dot(swap, stacked, preferred_element_type=F32).astype(BF16)
    return jnp.concatenate(
        [
            jnp.concatenate(
                [
                    moved[j * line:(j + 1) * line, g * LANES:(g + 1) * LANES]
                    for j in range(blocks)
                ],
                axis=1,
            )
            for g in range(groups)
        ],
        axis=0,
    )


def kernel(
    experts, halves,
    tokens_ref, router_ref, w_in_ref, w_out_ref, out_ref,
    tok, rout, first, second, send, recv, part, ret, mixed,
    in_sems, out_sems, send_sems, recv_sems,
):
    devices = experts * halves
    me_e, me_h = lax.axis_index("expert"), lax.axis_index("half")
    me = me_e * halves + me_h
    patches, width = tok.shape
    blocks = width // LANES

    loads = [
        pltpu.make_async_copy(src, dst, in_sems.at[k])
        for k, (src, dst) in enumerate(
            [(tokens_ref, tok), (router_ref, rout), (w_in_ref.at[0], first), (w_out_ref.at[0], second)]
        )
    ]
    for load in loads:
        load.start()

    def others(act):
        for dh in range(1, halves):
            act(me_e, lax.rem(me_h + dh, halves))

        @pl.loop(1, experts)
        def _(de):
            e = lax.rem(me_e + de, experts)
            for dh in range(halves):
                act(e, lax.rem(me_h + dh, halves))

    barrier = pltpu.get_barrier_semaphore()
    others(lambda e, h: pl.semaphore_signal(barrier, inc=1, device_id=(e, h), device_id_type=MESH))

    swap = swap_matrix(blocks)

    loads[0].wait()
    loads[1].wait()
    logits = lax.dot_general(
        rout[...], tok[...], (((1,), (1,)), ((), ())), preferred_element_type=F32
    )
    up = jnp.exp(logits - jnp.max(logits, axis=1, keepdims=True))
    dispatch = (up / jnp.sum(up, axis=1, keepdims=True)).astype(BF16)
    slot_input = jnp.dot(dispatch, tok[...], preferred_element_type=F32).astype(BF16)
    for g, tiles in enumerate(to_messages(swap, slot_input, blocks)):
        send[g * blocks:(g + 1) * blocks] = tiles

    pl.semaphore_wait(barrier, devices - 1)

    def dispatch_to(e, h):
        pltpu.make_async_remote_copy(
            src_ref=send.at[e], dst_ref=recv.at[me],
            send_sem=send_sems.at[0], recv_sem=recv_sems.at[0],
            device_id=(e, h), device_id_type=MESH,
        ).start()

    others(dispatch_to)
    pltpu.make_async_copy(send.at[me_e], recv.at[me], recv_sems.at[0]).start()

    across = jnp.exp(logits - jnp.max(logits, axis=0, keepdims=True))
    combine = (across / jnp.sum(across, axis=0, keepdims=True)).astype(F32)
    combine = combine.T.astype(BF16)

    loads[2].wait()
    loads[3].wait()
    pltpu.make_async_copy(recv, recv, recv_sems.at[0]).wait()

    rows = to_rows(swap, recv[...], blocks)
    hidden = jax.nn.gelu(jnp.dot(rows, first[...], preferred_element_type=F32)).astype(BF16)
    terms = jnp.dot(hidden, second[...], preferred_element_type=F32).astype(BF16)
    for g, tiles in enumerate(to_messages(swap, terms, blocks)):
        part[g * blocks:(g + 1) * blocks] = tiles

    place = me_h * experts + me_e

    def return_to(e, h):
        pltpu.make_async_remote_copy(
            src_ref=part.at[e * halves + h], dst_ref=ret.at[place],
            send_sem=send_sems.at[1], recv_sem=recv_sems.at[1],
            device_id=(e, h), device_id_type=MESH,
        ).start()

    others(return_to)
    pltpu.make_async_copy(part.at[me], ret.at[place], recv_sems.at[1]).start()
    pltpu.make_async_copy(ret, ret, recv_sems.at[1]).wait()

    total = ret[0:experts].astype(F32)
    for h in range(1, halves):
        total = total + ret[h * experts:(h + 1) * experts].astype(F32)
    slot_output = to_rows(swap, total.astype(BF16), blocks)

    chunks = 4
    chunk = patches // chunks
    stores = []
    for k in range(chunks):
        span = pl.ds(k * chunk, chunk)
        mixed[span, :] = jnp.dot(
            combine[k * chunk:(k + 1) * chunk], slot_output, preferred_element_type=F32
        ).astype(BF16)
        store = pltpu.make_async_copy(mixed.at[span], out_ref.at[span], out_sems.at[k])
        store.start()
        stores.append(store)

    sent = recv.at[pl.ds(0, devices - 1)]
    for k in range(2):
        pltpu.make_async_copy(sent, sent, send_sems.at[k]).wait()
    for store in stores:
        store.wait()


def solution(mesh):
    experts, halves = mesh.shape["expert"], mesh.shape["half"]
    devices = experts * halves

    def on_device(tokens, router, w_in, w_out):
        patches, width = tokens.shape
        share = w_in.shape[2]
        columns = router.shape[1]
        tile = (SLOTS * width // LANES, LANES)
        dma = pltpu.SemaphoreType.DMA
        return pl.pallas_call(
            functools.partial(kernel, experts, halves),
            out_shape=jax.ShapeDtypeStruct((patches, width), BF16),
            in_specs=[pl.BlockSpec(memory_space=pl.ANY)] * 4,
            out_specs=pl.BlockSpec(memory_space=pl.ANY),
            scratch_shapes=[
                pltpu.VMEM((patches, width), BF16),
                pltpu.VMEM((columns, width), BF16),
                pltpu.VMEM((width, share), BF16),
                pltpu.VMEM((share, width), BF16),
                pltpu.VMEM((experts, *tile), BF16),
                pltpu.VMEM((devices, *tile), BF16),
                pltpu.VMEM((devices, *tile), BF16),
                pltpu.VMEM((devices, *tile), BF16),
                pltpu.VMEM((patches, width), BF16),
                dma((4,)),
                dma((4,)),
                dma((2,)),
                dma((2,)),
            ],
            compiler_params=pltpu.CompilerParams(
                collective_id=0, has_side_effects=True, vmem_limit_bytes=56 * 2**20
            ),
            name="soft_moe",
        )(tokens, router.T, w_in, w_out)

    return jax.shard_map(
        on_device,
        mesh=mesh,
        in_specs=(
            P(("expert", "half"), None),
            P(),
            P("expert", None, "half"),
            P("expert", "half", None),
        ),
        out_specs=P(("expert", "half"), None),
        check_vma=False,
    )
```

time: 70 us -> 21.7 us (0.31)
  blocking collectives: 31.2 us -> 0 us
  Pallas kernels: 0 us -> 19.7 us
  waiting for transfers between devices: 17.2 us -> 0 us
  between operations: 13.4 us -> 0.01 us
  matrix products: 6.84 us -> 0 us
  local copies, waits for them, and re-layouts: 0.84 us -> 1.87 us
    all_to_all x2 -> x0, blocking collectives: 25.7 us -> none  [the longest x1 13.7 us: on_device(): lax.all_to_all(outgoing, 'expert', split_axis=1, concat_axis=0, tiled=True)]
    pallas_call x0 -> x1, Pallas kernels: none -> 19.7 us  [on_device(): pl.pallas_call(functools.partial(kernel, experts, halves), out_shape=jax....]
    reduce_scatter x1 -> x0, waiting for transfers between devices: 17.2 us -> none  [on_device(): lax.psum_scatter(terms.astype(jnp.bfloat16), 'half', scatter_dimension=1,...]
    dot_general x4 -> x0, matrix products: 6.84 us -> none  [the longest x1 2.91 us: expert_quarter(): jnp.einsum('erf,efd->erd', hidden, second, preferred_element_type=jnp.flo...]
    all_gather x1 -> x0, blocking collectives: 5.43 us -> none  [on_device(): lax.all_gather(slot_rows_local, 'half', axis=1, tiled=True)]
    unnamed x2 -> x1, local copies, waits for them, and re-layouts: 0.01 us -> 1.87 us
    another operation x3 -> x0, local copies, waits for them, and re-layouts: 0.81 us -> none  [the longest x1 0.77 us: on_device(): jnp.transpose(result.reshape(local_experts, -1, SLOTS, width), (1, 0, 2, 3))]
  transfers between devices with their start and end apart: 1 -> 0, of which waited for: 1 -> 0; matrix products, arithmetic and copies ran while one was open for 0% -> 0% of each run, Pallas kernels for 0% -> 0%
where the time goes in v1:
time: 21.7 us; the launch traced here: 21.6 us
  Pallas kernels  19.7 us (91%)
  local copies, waits for them, and re-layouts  1.87 us (9%)
    pallas_call x1, Pallas kernels, on_device(): pl.pallas_call(functools.partial(kernel, experts, halves), out_shape=jax....  19.7 us
    unnamed x1, local copies, waits for them, and re-layouts  1.87 us

profile of v1, /device:TPU:0, one launch (start us, length us, event | category | flops | bytes accessed | tf_op | source)
XLA Modules:
  0.0 21.6 jit_solution(8025712210646347700)
XLA Ops:
  0.0 19.7 %soft_moe.1 = bf16[256,1024]{1,0:T(8,128)(2,1)} custom-call(bf16[256,1024]{1,0:T(8,128)(2,1)} %tokens_ref.1, bf16[16,1024]{1,0:T(8,128)(2,1)} %bitcast.1, bf16[1,1024,768]{2,1,0:T(8,128)(2,1)} %w_in_ref.1, bf16[1,768,1024]{2,1,0:T(8,128)(2,1)} %w_out_ref.1), custom_call_target="tpu_custom_call" | custom-call | tf_op jit(solution)/shard_map/soft_moe/pallas_call | solution.py:191
  19.7 1.9 %copy.6 = bf16[256,1024]{1,0:T(8,128)(2,1)} copy(bf16[256,1024]{1,0:T(8,128)(2,1)} %soft_moe.1) | data formatting | bytes 1048576

commit v2 on v1

--- a/solution.py
+++ b/solution.py
@@ -68,11 +68,36 @@
     )
 
 
+def mix_kernel(combine_ref, slots_ref, out_ref, mixed, sems):
+    combine = combine_ref[...].astype(F32).T.astype(BF16)
+    chunks = sems.shape[0]
+    chunk = mixed.shape[0] // chunks
+    stores = []
+    for k in range(chunks):
+        span = pl.ds(k * chunk, chunk)
+        mixed[span, :] = jnp.dot(
+            combine[k * chunk:(k + 1) * chunk], slots_ref[...], preferred_element_type=F32
+        ).astype(BF16)
+        store = pltpu.make_async_copy(mixed.at[span], out_ref.at[span], sems.at[k])
+        store.start()
+        stores.append(store)
+    for store in stores:
+        store.wait()
+
+
+def exclusive_or(a, b, size):
+    value, bit = 0, 1
+    while bit < size:
+        value = value + bit * lax.rem(lax.div(a, bit) + lax.div(b, bit), 2)
+        bit *= 2
+    return value
+
+
 def kernel(
     experts, halves,
-    tokens_ref, router_ref, w_in_ref, w_out_ref, out_ref,
-    tok, rout, first, second, send, recv, part, ret, mixed,
-    in_sems, out_sems, send_sems, recv_sems,
+    tokens_ref, router_ref, w_in_ref, w_out_ref, mixed_rows, combine_out,
+    tok, rout, first, second, send, recv, part, ret,
+    in_sems, send_sems, recv_sems,
 ):
     devices = experts * halves
     me_e, me_h = lax.axis_index("expert"), lax.axis_index("half")
@@ -86,21 +111,25 @@
             [(tokens_ref, tok), (router_ref, rout), (w_in_ref.at[0], first), (w_out_ref.at[0], second)]
         )
     ]
-    for load in loads:
-        load.start()
+    loads[0].start()
+    loads[1].start()
+
+    order = [exclusive_or(me_h, jnp.int32(d), halves) for d in reversed(range(halves))]
 
     def others(act):
-        for dh in range(1, halves):
-            act(me_e, lax.rem(me_h + dh, halves))
-
         @pl.loop(1, experts)
-        def _(de):
-            e = lax.rem(me_e + de, experts)
-            for dh in range(halves):
-                act(e, lax.rem(me_h + dh, halves))
+        def _(k):
+            e = exclusive_or(me_e, experts - k, experts)
+            for h in order:
+                act(e, h)
+
+        for h in order[:-1]:
+            act(me_e, h)
 
     barrier = pltpu.get_barrier_semaphore()
     others(lambda e, h: pl.semaphore_signal(barrier, inc=1, device_id=(e, h), device_id_type=MESH))
+    loads[2].start()
+    loads[3].start()
 
     swap = swap_matrix(blocks)
 
@@ -128,8 +157,7 @@
     pltpu.make_async_copy(send.at[me_e], recv.at[me], recv_sems.at[0]).start()
 
     across = jnp.exp(logits - jnp.max(logits, axis=0, keepdims=True))
-    combine = (across / jnp.sum(across, axis=0, keepdims=True)).astype(F32)
-    combine = combine.T.astype(BF16)
+    combine_t = (across / jnp.sum(across, axis=0, keepdims=True)).astype(BF16)
 
     loads[2].wait()
     loads[3].wait()
@@ -159,23 +187,12 @@
         total = total + ret[h * experts:(h + 1) * experts].astype(F32)
     slot_output = to_rows(swap, total.astype(BF16), blocks)
 
-    chunks = 4
-    chunk = patches // chunks
-    stores = []
-    for k in range(chunks):
-        span = pl.ds(k * chunk, chunk)
-        mixed[span, :] = jnp.dot(
-            combine[k * chunk:(k + 1) * chunk], slot_output, preferred_element_type=F32
-        ).astype(BF16)
-        store = pltpu.make_async_copy(mixed.at[span], out_ref.at[span], out_sems.at[k])
-        store.start()
-        stores.append(store)
+    mixed_rows[...] = slot_output
+    combine_out[...] = combine_t
 
     sent = recv.at[pl.ds(0, devices - 1)]
     for k in range(2):
         pltpu.make_async_copy(sent, sent, send_sems.at[k]).wait()
-    for store in stores:
-        store.wait()
 
 
 def solution(mesh):
@@ -188,11 +205,11 @@
         columns = router.shape[1]
         tile = (SLOTS * width // LANES, LANES)
         dma = pltpu.SemaphoreType.DMA
-        return pl.pallas_call(
+        slot_output, combine = pl.pallas_call(
             functools.partial(kernel, experts, halves),
-            out_shape=jax.ShapeDtypeStruct((patches, width), BF16),
-            in_specs=[pl.BlockSpec(memory_space=pl.ANY)] * 4,
-            out_specs=pl.BlockSpec(memory_space=pl.ANY),
+            out_shape=[jax.ShapeDtypeStruct((columns, width), BF16), jax.ShapeDtypeStruct((columns, patches), BF16)],
+            in_specs=[pl.BlockSpec(memory_space=pltpu.HBM)] * 4,
+            out_specs=[pl.BlockSpec(memory_space=pltpu.VMEM)] * 2,
             scratch_shapes=[
                 pltpu.VMEM((patches, width), BF16),
                 pltpu.VMEM((columns, width), BF16),
@@ -202,17 +219,24 @@
                 pltpu.VMEM((devices, *tile), BF16),
                 pltpu.VMEM((devices, *tile), BF16),
                 pltpu.VMEM((devices, *tile), BF16),
-                pltpu.VMEM((patches, width), BF16),
-                dma((4,)),
                 dma((4,)),
                 dma((2,)),
                 dma((2,)),
             ],
             compiler_params=pltpu.CompilerParams(
-                collective_id=0, has_side_effects=True, vmem_limit_bytes=56 * 2**20
+                collective_id=0, has_side_effects=True, vmem_limit_bytes=55168 * 2**10
             ),
             name="soft_moe",
         )(tokens, router.T, w_in, w_out)
+        return pl.pallas_call(
+            mix_kernel,
+            out_shape=jax.ShapeDtypeStruct((patches, width), BF16),
+            in_specs=[pl.BlockSpec(memory_space=pltpu.VMEM)] * 2,
+            out_specs=pl.BlockSpec(memory_space=pl.ANY),
+            scratch_shapes=[pltpu.VMEM((patches, width), BF16), dma((4,))],
+            compiler_params=pltpu.CompilerParams(vmem_limit_bytes=16 * 2**20),
+            name="mix",
+        )(combine, slot_output)
 
     return jax.shard_map(
         on_device,

time: 21.7 us -> 19.8 us (0.912)
  local copies, waits for them, and re-layouts: 1.87 us -> 0 us
    unnamed x1 -> x0, local copies, waits for them, and re-layouts: 1.87 us -> none
    pallas_call x1 -> x2, Pallas kernels: 19.7 us -> 19.6 us  [the longest x1 18.6 us: on_device(): pl.pallas_call(functools.partial(kernel, experts, halves), out_shape=[jax...]
where the time goes in v2:
time: 19.8 us; the launch traced here: 19.7 us
  Pallas kernels  19.6 us (99%)
    pallas_call x1, Pallas kernels, on_device(): pl.pallas_call(functools.partial(kernel, experts, halves), out_shape=[jax...  18.6 us
    pallas_call x1, Pallas kernels, on_device(): pl.pallas_call(mix_kernel, out_shape=jax.ShapeDtypeStruct((patches, width...  1.05 us

profile of v2, /device:TPU:0, one launch (start us, length us, event | category | flops | bytes accessed | tf_op | source)
XLA Modules:
  0.0 19.7 jit_solution(10249527134048190354)
XLA Ops:
  0.0 18.6 %soft_moe.1 = (bf16[16,1024]{1,0:T(8,128)(2,1)S(1)}, bf16[16,256]{1,0:T(8,128)(2,1)S(1)}) custom-call(bf16[256,1024]{1,0:T(8,128)(2,1)} %tokens_ref.1, bf16[16,1024]{1,0:T(8,128)(2,1)} %bitcast.1, bf16[1,1024,768]{2,1,0:T(8,128)(2,1)} %w_in_ref.1, bf16[1,768,1024]{2,1,0:T(8,128)(2,1)} %w_out_ref.1), custom_call_target="tpu_custom_call" | custom-call | tf_op jit(solution)/shard_map/soft_moe/pallas_call | solution.py:208
  18.6 1.1 %mix.1 = bf16[256,1024]{1,0:T(8,128)(2,1)} custom-call(bf16[16,256]{1,0:T(8,128)(2,1)S(1)} %get-tuple-element.7.combine_ref, bf16[16,1024]{1,0:T(8,128)(2,1)S(1)} %get-tuple-element.8.slots_ref), custom_call_target="tpu_custom_call" | custom-call | tf_op jit(solution)/shard_map/mix/pallas_call | solution.py:231
